TPU v7x, 32 devices: a whole 2x2x4 slice. The times are simulated.
32 devices in a mesh: dp: 2 (over y), expert: 16 (over z, x, core).
Axes of the slice: x: 2, y: 2, z: 4, core: 2. Of those that a mesh axis runs over, the one named last changes fastest.
Arguments:
- activations: bfloat16 [4096, 4096], P(('dp', 'expert')), may hold values from -6 to 6
- cotangent: bfloat16 [4096, 4096], P(('dp', 'expert')), may hold values from -6 to 6
- expert_ids: int32 [4096, 1], P(('dp', 'expert')), may hold values from 0 to 127; in each aligned block of 128 rows (0 to 127, 128 to 255, ...) at most 2 rows name the same one
- gate_probs: float32 [4096, 1], P(('dp', 'expert')), may hold values from 0.2 to 1
- gate_up: bfloat16 [16, 2, 4096, 1536], P('expert', None, None, 'dp'), may hold values from -0.09375 to 0.09375
- down_proj: bfloat16 [16, 1536, 4096], P('expert', 'dp'), may hold values from -0.15625 to 0.15625
Outputs:
- input_grad: bfloat16 [4096, 4096], P(('dp', 'expert'))
- grad_gate_up: bfloat16 [16, 2, 4096, 1536], P('expert', None, None, 'dp')
- grad_down: bfloat16 [16, 1536, 4096], P('expert', 'dp')
Inputs may be any that keep to these rules, and one draw needn't show every extreme that they name: `expert_ids`: expert e < 16 is held by index e of the expert axis. Among the 128 tokens of one device no expert is named more than 2 times, a bound that some block reaches.
All inputs are finite; a program needn't handle non-finite values.
Results may differ from a plain program's by a relative error of at most 0.0058.
Values may be sent and summed in bfloat16 or wider, within the bound.
No kernel may reach another device: no remote copies, remote signals or barrier semaphores. Data moves between devices by JAX's collectives and lax.ppermute only.
A program may use at most 128 MiB of HBM per device.

v0:
```python
import jax
import jax.numpy as jnp
from jax import lax
from jax.sharding import PartitionSpec as P

CAP = 2


def contract(left, right, left_dim, right_dim):
    return lax.dot_general(
        left, right, (((left_dim,), (right_dim,)), ((), ())), preferred_element_type=jnp.float32
    )


def block_backward(rows_tok, rows_cot, pair_weights, down_weights):
    pre_gate = jnp.dot(rows_tok, pair_weights[0], preferred_element_type=jnp.float32)
    pre_up = jnp.dot(rows_tok, pair_weights[1], preferred_element_type=jnp.float32)
    sigmoid_gate = jax.nn.sigmoid(pre_gate)
    activated = pre_gate * sigmoid_gate
    hidden = (activated * pre_up).astype(jnp.bfloat16)
    hidden_grad = contract(rows_cot, down_weights, 1, 1)
    gate_grad = (
        hidden_grad * pre_up * sigmoid_gate * (1.0 + pre_gate * (1.0 - sigmoid_gate))
    ).astype(jnp.bfloat16)
    up_grad = (hidden_grad * activated).astype(jnp.bfloat16)
    total_down = contract(hidden, rows_cot, 0, 0)
    total_gate = contract(rows_tok, gate_grad, 0, 0)
    total_up = contract(rows_tok, up_grad, 0, 0)
    input_rows = contract(gate_grad, pair_weights[0], 1, 1) + contract(
        up_grad, pair_weights[1], 1, 1
    )
    return (total_gate, total_up, total_down, input_rows)


def expert_rows(rows_tok, rows_cot, pair_weights, down_weights):
    row_count = rows_tok.shape[0]
    block_rows = min(256, row_count)
    model_width = rows_tok.shape[1]
    unit_count = down_weights.shape[0]
    block_count = row_count // block_rows

    def advance(counter, carry_state):
        total_gate, total_up, total_down, input_all = carry_state
        part_tok = lax.dynamic_slice_in_dim(rows_tok, counter * block_rows, block_rows)
        part_cot = lax.dynamic_slice_in_dim(rows_cot, counter * block_rows, block_rows)
        more_gate, more_up, more_down, input_rows = block_backward(
            part_tok, part_cot, pair_weights, down_weights
        )
        input_all = lax.dynamic_update_slice_in_dim(input_all, input_rows, counter * block_rows, 0)
        return (total_gate + more_gate, total_up + more_up, total_down + more_down, input_all)

    initial = (
        jnp.zeros((model_width, unit_count), jnp.float32),
        jnp.zeros((model_width, unit_count), jnp.float32),
        jnp.zeros((unit_count, model_width), jnp.float32),
        jnp.zeros((row_count, model_width), jnp.float32),
    )
    total_gate, total_up, total_down, input_all = lax.fori_loop(0, block_count, advance, initial)
    return (jnp.stack([total_gate, total_up]), total_down, input_all)


def per_device(activations, cotangent, expert_ids, gate_probs, gate_up, down_proj):
    experts = lax.axis_size("expert")
    identity = expert_ids[:, 0]
    in_window = identity < experts
    onehot = (identity[:, None] == jnp.arange(experts, dtype=jnp.int32)[None, :]).astype(jnp.int32)
    before = jnp.cumsum(onehot, axis=0) - onehot
    ranking = jnp.sum(before * onehot, axis=1)
    slot_index = identity * CAP + ranking
    slot_index = jnp.where(in_window, slot_index, -1)
    placing = (slot_index[None, :] == jnp.arange(experts * CAP, dtype=jnp.int32)[:, None]).astype(
        jnp.bfloat16
    )
    scaled = (gate_probs * cotangent.astype(jnp.float32)).astype(jnp.bfloat16)
    send_tok = jnp.dot(placing, activations, preferred_element_type=jnp.float32).astype(
        jnp.bfloat16
    )
    send_cot = jnp.dot(placing, scaled, preferred_element_type=jnp.float32).astype(jnp.bfloat16)
    got_tok, got_cot = (
        lax.all_to_all(send_tok, "expert", split_axis=0, concat_axis=0, tiled=True),
        lax.all_to_all(send_cot, "expert", split_axis=0, concat_axis=0, tiled=True),
    )
    all_tok, all_cot = (
        lax.all_gather(got_tok, "dp", axis=0, tiled=True),
        lax.all_gather(got_cot, "dp", axis=0, tiled=True),
    )
    own_pair = gate_up[0]
    own_down = down_proj[0]
    pair_total, down_total, partial_value = expert_rows(all_tok, all_cot, own_pair, own_down)
    summed = lax.psum_scatter(partial_value, "dp", scatter_dimension=0, tiled=True)
    rounded = summed.astype(jnp.bfloat16)
    returned = lax.all_to_all(rounded, "expert", split_axis=0, concat_axis=0, tiled=True)
    input_grad = contract(placing, returned, 0, 0).astype(jnp.bfloat16)
    return (
        input_grad,
        pair_total[None].astype(jnp.bfloat16),
        down_total[None].astype(jnp.bfloat16),
    )


def solution(mesh):
    in_specs = (
        P(("dp", "expert"), None),
        P(("dp", "expert"), None),
        P(("dp", "expert"), None),
        P(("dp", "expert"), None),
        P("expert", None, None, "dp"),
        P("expert", "dp", None),
    )
    out_specs = (P(("dp", "expert"), None), P("expert", None, None, "dp"), P("expert", "dp", None))
    return jax.shard_map(
        per_device, mesh=mesh, in_specs=in_specs, out_specs=out_specs, check_vma=False
    )
```

profile of v0, /device:TPU:0, one launch (start us, length us, event | category | flops | bytes accessed | tf_op | source)
XLA Modules:
  0.0 121.2 jit_solution(6913211261326391210)
XLA Ops:
  7.2 0.8 fusion.22
  8.2 0.8 select_reduce_fusion
  10.0 0.9 all_to_all.27
  10.8 7.4 %all-to-all-start.1 = ((bf16[16,2,4096]{2,1,0:T(2,128)(2,1)}), bf16[16,2,4096]{2,1,0:T(2,128)(2,1)S(1)}, u32[]{:S(2)}, u32[]{:S(2)}) async-start(bf16[16,2,4096]{2,1,0:T(2,128)(2,1)} %all_to_all.27), calls=%async_computation.1 | async-start | bytes 524288 | tf_op jit(solution)/shard_map/all_to_all | solution.py:80
  18.2 1.6 %convolution_convert_fusion.5 = bf16[32,4096]{1,0:T(8,128)(2,1)S(1)} fusion(bf16[128,4096]{1,0:T(8,128)(2,1)} %param.7, f32[128]{0:T(128)} %bitcast.40, s32[128]{0:T(128)S(1)} %compare_select_fusion), kind=kOutput, calls=%fused_computation.24 | convolution fusion | flops 35262464 | bytes 1311744 | tf_op jit(solution)/shard_map/dot_general | solution.py:78
  19.8 0.9 all_to_all.24
  20.7 7.5 %all-to-all-done.1 = bf16[16,2,4096]{2,1,0:T(2,128)(2,1)S(1)} async-done(((bf16[16,2,4096]{2,1,0:T(2,128)(2,1)}), bf16[16,2,4096]{2,1,0:T(2,128)(2,1)S(1)}, u32[]{:S(2)}, u32[]{:S(2)}) %all-to-all-start.1) | async-done | bytes 262176 | tf_op jit(solution)/shard_map/all_to_all | solution.py:80
  28.3 3.5 %all-to-all-start = ((bf16[16,2,4096]{2,1,0:T(2,128)(2,1)}), bf16[16,2,4096]{2,1,0:T(2,128)(2,1)S(1)}, u32[]{:S(2)}, u32[]{:S(2)}) async-start(bf16[16,2,4096]{2,1,0:T(2,128)(2,1)} %all_to_all.24), calls=%async_computation | async-start | bytes 524288 | tf_op jit(solution)/shard_map/all_to_all | solution.py:81
  32.0 9.2 %all_gather.7 = bf16[64,4096]{1,0:T(8,128)(2,1)S(1)} all-gather(bf16[32,4096]{1,0:T(8,128)(2,1)S(1)} %all_to_all.29), channel_id=1, replica_groups=mesh['dp'=2,'expert'=16] {'dp'}, dimensions={0}, use_global_device_ids=true | all-gather | bytes 786432 | tf_op jit(solution)/shard_map/all_gather | solution.py:84
  41.1 4.0 %fusion.2 = f32[64,768]{1,0:T(8,128)S(1)} fusion(bf16[64,4096]{1,0:T(8,128)(2,1)S(1)} %all_gather.7, bf16[1,2,4096,768]{3,2,1,0:T(8,128)(2,1)} %param.10), kind=kOutput, calls=%fused_computation.6 | convolution fusion | flops 402653184 | bytes 7012352 | tf_op jit(solution)/shard_map/while/body/eval_jaxpr/dot_general | solution.py:16
  45.1 4.0 %fusion.6 = f32[64,768]{1,0:T(8,128)S(1)} fusion(bf16[64,4096]{1,0:T(8,128)(2,1)S(1)} %all_gather.7, bf16[1,2,4096,768]{3,2,1,0:T(8,128)(2,1)} %param.10), kind=kOutput, calls=%fused_computation.10 | convolution fusion | flops 402653184 | bytes 7012352 | tf_op jit(solution)/shard_map/while/body/eval_jaxpr/dot_general | solution.py:17
  49.2 8.5 %all_gather.6 = bf16[64,4096]{1,0:T(8,128)(2,1)S(1)} all-gather(bf16[32,4096]{1,0:T(8,128)(2,1)S(1)} %all_to_all.26), channel_id=1, replica_groups=mesh['dp'=2,'expert'=16] {'dp'}, dimensions={0}, use_global_device_ids=true | all-gather | bytes 786432 | tf_op jit(solution)/shard_map/all_gather | solution.py:85
  57.7 4.8 %multiply_convert_fusion.3 = (bf16[64,768]{1,0:T(8,128)(2,1)S(1)}, bf16[64,768]{1,0:T(8,128)(2,1)S(1)}) fusion(f32[64,768]{1,0:T(8,128)S(1)} %fusion.2, f32[64,768]{1,0:T(8,128)S(1)} %fusion.6, bf16[64,4096]{1,0:T(8,128)(2,1)S(1)} %all_gather.6, bf16[1,768,4096]{2,1,0:T(8,128)(2,1)} %param.11), kind=kOutput, calls=%fused_computation.28 | convolution fusion | flops 403292160 | bytes 7405568 | tf_op jit(solution)/shard_map/while/body/eval_jaxpr/dot_general | solution.py:10
  62.6 4.8 %fusion = f32[64,4096]{1,0:T(8,128)S(1)} fusion(bf16[64,768]{1,0:T(8,128)(2,1)S(1)} %get-tuple-element.24, bf16[1,2,4096,768]{3,2,1,0:T(8,128)(2,1)} %param.10), kind=kOutput, calls=%fused_computation.4 | convolution fusion | flops 402653184 | bytes 7438336 | tf_op jit(solution)/shard_map/while/body/eval_jaxpr/dot_general | solution.py:10
  67.4 5.8 %fusion.17 = f32[64,4096]{1,0:T(8,128)} fusion(f32[64,4096]{1,0:T(8,128)S(1)} %fusion, bf16[64,768]{1,0:T(8,128)(2,1)S(1)} %get-tuple-element.23, bf16[1,2,4096,768]{3,2,1,0:T(8,128)(2,1)} %param.10), kind=kOutput, calls=%fused_computation.22 | convolution fusion | flops 402915328 | bytes 8486912 | tf_op jit(solution)/shard_map/while/body/eval_jaxpr/dot_general | solution.py:10
  73.2 4.5 %fusion.10 = bf16[1,1,4096,768]{3,2,1,0:T(8,128)(2,1)} fusion(bf16[64,4096]{1,0:T(8,128)(2,1)S(1)} %all_gather.7, bf16[64,768]{1,0:T(8,128)(2,1)S(1)} %get-tuple-element.24), kind=kOutput, calls=%fused_computation.14 | convolution fusion | flops 405798912 | bytes 6914048 | tf_op jit(solution)/shard_map/while/body/eval_jaxpr/dot_general | solution.py:10
  77.7 4.5 %fusion.11 = bf16[1,1,4096,768]{3,2,1,0:T(8,128)(2,1)} fusion(bf16[64,4096]{1,0:T(8,128)(2,1)S(1)} %all_gather.7, bf16[64,768]{1,0:T(8,128)(2,1)S(1)} %get-tuple-element.23), kind=kOutput, calls=%fused_computation.15 | convolution fusion | flops 405798912 | bytes 6914048 | tf_op jit(solution)/shard_map/while/body/eval_jaxpr/dot_general | solution.py:10
  82.2 4.5 %fusion.12 = bf16[1,768,4096]{2,1,0:T(8,128)(2,1)} fusion(bf16[64,4096]{1,0:T(8,128)(2,1)S(1)} %all_gather.6, f32[64,768]{1,0:T(8,128)S(1)} %fusion.6, f32[64,768]{1,0:T(8,128)S(1)} %fusion.2), kind=kOutput, calls=%fused_computation.16 | convolution fusion | flops 406093824 | bytes 7208960 | tf_op jit(solution)/shard_map/while/body/eval_jaxpr/dot_general | solution.py:10
  86.7 8.0 %reduce-scatter.2.cloned.1.call-done = f32[32,4096]{1,0:T(8,128)} async-done(((f32[64,4096]{1,0:T(8,128)}), f32[32,4096]{1,0:T(8,128)}) %reduce-scatter.2.cloned.1.call-update) | async-done | bytes 524304 | tf_op jit(solution)/shard_map/reduce_scatter | solution.py:90
  94.7 1.1 convert_element_type.56
  95.7 0.9 all_to_all.30
  96.6 5.6 %all-to-all-start.2 = ((bf16[16,2,4096]{2,1,0:T(2,128)(2,1)}), bf16[16,2,4096]{2,1,0:T(2,128)(2,1)S(1)}, u32[]{:S(2)}, u32[]{:S(2)}) async-start(bf16[16,2,4096]{2,1,0:T(2,128)(2,1)} %all_to_all.30), calls=%async_computation.3 | async-start | bytes 524288 | tf_op jit(solution)/shard_map/all_to_all | solution.py:92
  102.2 10.5 %pad_maximum_fusion = bf16[1,2,4096,768]{3,2,1,0:T(8,128)(2,1)} fusion(bf16[1,1,4096,768]{3,2,1,0:T(8,128)(2,1)} %fusion.11, bf16[1,1,4096,768]{3,2,1,0:T(8,128)(2,1)} %fusion.10), kind=kLoop, calls=%fused_computation | loop fusion | flops 6291456 | bytes 25165824 | tf_op jit(solution)/shard_map/stack | solution.py:59
  112.9 1.5 %convolution_convert_fusion.3 = bf16[128,4096]{1,0:T(8,128)(2,1)} fusion(bf16[32,4096]{1,0:T(8,128)(2,1)S(1)} %all_to_all.32, s32[128]{0:T(128)S(1)} %compare_select_fusion), kind=kOutput, calls=%fused_computation.21 | convolution fusion | flops 34082816 | bytes 1311232 | tf_op jit(solution)/shard_map/dot_general | solution.py:10
  (12 shorter events, 1.5 us)
Async XLA Ops:
  7.2 2.5 %copy-start = (bf16[128,4096]{1,0:T(8,128)(2,1)S(1)}, bf16[128,4096]{1,0:T(8,128)(2,1)}, u32[]{:S(2)}) copy-start(bf16[128,4096]{1,0:T(8,128)(2,1)} %param.6) | copy-start | bytes 3145732
  10.8 17.4 %all-to-all-start.1 = ((bf16[16,2,4096]{2,1,0:T(2,128)(2,1)}), bf16[16,2,4096]{2,1,0:T(2,128)(2,1)S(1)}, u32[]{:S(2)}, u32[]{:S(2)}) async-start(bf16[16,2,4096]{2,1,0:T(2,128)(2,1)} %all_to_all.27), calls=%async_computation.1 | async-start | bytes 524288 | tf_op jit(solution)/shard_map/all_to_all | solution.py:80
  28.3 20.8 %all-to-all-start = ((bf16[16,2,4096]{2,1,0:T(2,128)(2,1)}), bf16[16,2,4096]{2,1,0:T(2,128)(2,1)S(1)}, u32[]{:S(2)}, u32[]{:S(2)}) async-start(bf16[16,2,4096]{2,1,0:T(2,128)(2,1)} %all_to_all.24), calls=%async_computation | async-start | bytes 524288 | tf_op jit(solution)/shard_map/all_to_all | solution.py:81
  31.8 62.9 %reduce-scatter.2.cloned.1.call-start = ((), (), s32[]{:S(2)}) async-start(), calls=%async_computation.4 | async-start | bytes 1572864 | tf_op jit(solution)/shard_map/reduce_scatter | solution.py:90
  96.6 16.2 %all-to-all-start.2 = ((bf16[16,2,4096]{2,1,0:T(2,128)(2,1)}), bf16[16,2,4096]{2,1,0:T(2,128)(2,1)S(1)}, u32[]{:S(2)}, u32[]{:S(2)}) async-start(bf16[16,2,4096]{2,1,0:T(2,128)(2,1)} %all_to_all.30), calls=%async_computation.3 | async-start | bytes 524288 | tf_op jit(solution)/shard_map/all_to_all | solution.py:92
Sparse Core Ops, SparseCore 0:
  73.3 21.3 reduce-scatter.1
where the time goes:
time: 122 us; the launch traced here: 121 us
  matrix products  40.2 us (33%)
  blocking collectives  17.7 us (15%)
  starting transfers between devices  16.6 us (14%)
  waiting for transfers between devices  15.5 us (13%)
  other arithmetic  14.1 us (12%)
  between operations  14.1 us (12%)
  local copies, waits for them, and re-layouts  2.98 us (2%)
    dot_general x7, matrix products, contract(): lax.dot_general(left, right, (((left_dim,), (right_dim,)), ((), ())), pre...  30.4 us
    another operation x1, other arithmetic, expert_rows(): return (jnp.stack([total_gate, total_up]), total_down, input_all)  10.5 us
    all_gather x1, blocking collectives, per_device(): lax.all_gather(got_tok, 'dp', axis=0, tiled=True)  9.17 us
    all_gather x1, blocking collectives, per_device(): lax.all_gather(got_cot, 'dp', axis=0, tiled=True)  8.54 us
    reduce_scatter x1, waiting for transfers between devices, per_device(): lax.psum_scatter(partial_value, 'dp', scatter_dimension=0, tiled=True)  7.96 us
    all_to_all x1, waiting for transfers between devices, per_device(): lax.all_to_all(send_tok, 'expert', split_axis=0, concat_axis=0, tiled=True)  7.55 us
    all_to_all x1, starting transfers between devices, per_device(): lax.all_to_all(send_tok, 'expert', split_axis=0, concat_axis=0, tiled=True)  7.36 us
    all_to_all x1, starting transfers between devices, per_device(): lax.all_to_all(rounded, 'expert', split_axis=0, concat_axis=0, tiled=True)  5.63 us
  transfers between devices with their start and end apart: 4, of which 2 were waited for; matrix products, arithmetic and copies ran while one was open for 28% of the time, Pallas kernels for 0%

commit v1 on v0

v1 whole, which is shorter than its diff:
```python
import functools

import jax
import jax.numpy as jnp
from jax import lax
from jax.experimental import pallas as pl
from jax.experimental.pallas import tpu as pltpu
from jax.sharding import PartitionSpec as P

CAP = 2
MIB = 1024 * 1024


def dot_nn(a, b):
    return lax.dot_general(a, b, (((1,), (0,)), ((), ())), preferred_element_type=jnp.float32)


def dot_nt(a, b):
    return lax.dot_general(a, b, (((1,), (1,)), ((), ())), preferred_element_type=jnp.float32)


def dot_tn(a, b):
    return lax.dot_general(a, b, (((0,), (0,)), ((), ())), preferred_element_type=jnp.float32)


def cost(flops, moved):
    return pl.CostEstimate(flops=int(flops), bytes_accessed=int(moved), transcendentals=0)


def route_kernel(experts, ids_ref, probs_ref, act_ref, cot_ref, send_ref, place_ref):
    ids = ids_ref[...]
    tokens = ids.shape[1]
    units = lax.broadcasted_iota(jnp.int32, (experts, tokens), 0)
    onehot = jnp.where(units == ids, 1.0, 0.0)
    earlier = lax.broadcasted_iota(jnp.int32, (tokens, tokens), 0) < lax.broadcasted_iota(
        jnp.int32, (tokens, tokens), 1
    )
    before = dot_nn(onehot.astype(jnp.bfloat16), jnp.where(earlier, 1.0, 0.0).astype(jnp.bfloat16))
    rank = jnp.sum(before * onehot, axis=0, keepdims=True).astype(jnp.int32)
    inside = ids < experts
    slot = jnp.where(inside, ids * CAP + rank, -1)
    slots = lax.broadcasted_iota(jnp.int32, (experts * CAP, tokens), 0)
    place_ref[...] = jnp.where(slots == slot, 1.0, 0.0).astype(jnp.bfloat16)
    wide = lax.broadcasted_iota(jnp.int32, (experts * 2 * CAP, tokens), 0)
    row = jnp.where(inside, ids * (2 * CAP) + rank, -2 * CAP)
    pick_tok = jnp.where(wide == row, 1.0, 0.0)
    pick_cot = jnp.where(wide == row + CAP, 1.0, 0.0)
    weight = jnp.sum(pick_cot * probs_ref[...], axis=1, keepdims=True)
    rows = dot_nn(pick_tok.astype(jnp.bfloat16), act_ref[...])
    rows = rows + weight * dot_nn(pick_cot.astype(jnp.bfloat16), cot_ref[...])
    rows = rows.astype(jnp.bfloat16)
    for unit in range(experts):
        send_ref[unit] = rows[unit * 2 * CAP : (unit + 1) * 2 * CAP]


def route(ids, probs, act, cot, experts):
    tokens, width = act.shape
    tile = min(1024, width)
    return pl.pallas_call(
        functools.partial(route_kernel, experts),
        grid=(width // tile,),
        in_specs=[
            pl.BlockSpec((1, tokens), lambda c: (0, 0)),
            pl.BlockSpec((1, tokens), lambda c: (0, 0)),
            pl.BlockSpec((tokens, tile), lambda c: (0, c)),
            pl.BlockSpec((tokens, tile), lambda c: (0, c)),
        ],
        out_specs=[
            pl.BlockSpec((experts, 2 * CAP, tile), lambda c: (0, 0, c)),
            pl.BlockSpec((experts * CAP, tokens), lambda c: (0, 0)),
        ],
        out_shape=[
            jax.ShapeDtypeStruct((experts, 2 * CAP, width), jnp.bfloat16),
            jax.ShapeDtypeStruct((experts * CAP, tokens), jnp.bfloat16),
        ],
        compiler_params=pltpu.CompilerParams(vmem_limit_bytes=16 * MIB),
        cost_estimate=cost(4 * experts * CAP * tokens * width, 4 * tokens * width),
        name="route_rows",
    )(ids, probs, act, cot)


def expert_kernel(groups, chunk, *refs):
    toks, cots = refs[:groups], refs[groups : 2 * groups]
    pair_hbm, down_hbm = refs[2 * groups : 2 * groups + 2]
    gate_out, up_out, hidden_out = refs[2 * groups + 2 : 2 * groups + 5]
    parts = refs[2 * groups + 5 : 3 * groups + 5]
    pair, down, tok_all, cot_all, acc_gate, acc_up, acc_hid, sems = refs[3 * groups + 5 :]
    rows, width = toks[0].shape
    steps = width // chunk

    def copies(step):
        at = pl.ds(step * chunk, chunk)
        return (
            pltpu.make_async_copy(pair_hbm.at[:, at, :], pair.at[:, at, :], sems.at[0, step]),
            pltpu.make_async_copy(down_hbm.at[:, at], down.at[:, at], sems.at[1, step]),
        )

    for step in range(steps):
        for one in copies(step):
            one.start()
    for group in range(groups):
        tok_all[group * rows : (group + 1) * rows, :] = toks[group][...]
        cot_all[group * rows : (group + 1) * rows, :] = cots[group][...]
    acc_gate[...] = jnp.zeros_like(acc_gate)
    acc_up[...] = jnp.zeros_like(acc_up)
    acc_hid[...] = jnp.zeros_like(acc_hid)

    for step in range(steps):
        at = slice(step * chunk, (step + 1) * chunk)
        for one in copies(step):
            one.wait()
        acc_gate[...] += dot_nn(tok_all[:, at], pair[0, at, :])
        acc_up[...] += dot_nn(tok_all[:, at], pair[1, at, :])
        acc_hid[...] += dot_nt(cot_all[:, at], down[:, at])

    pre_gate, pre_up, hidden_grad = acc_gate[...], acc_up[...], acc_hid[...]
    sigmoid_gate = jax.nn.sigmoid(pre_gate)
    activated = pre_gate * sigmoid_gate
    hidden_out[...] = (activated * pre_up).astype(jnp.bfloat16)
    gate_grad = (
        hidden_grad * pre_up * sigmoid_gate * (1.0 + pre_gate * (1.0 - sigmoid_gate))
    ).astype(jnp.bfloat16)
    up_grad = (hidden_grad * activated).astype(jnp.bfloat16)
    gate_out[...] = gate_grad
    up_out[...] = up_grad
    for step in range(steps):
        at = slice(step * chunk, (step + 1) * chunk)
        value = dot_nt(gate_grad, pair[0, at, :]) + dot_nt(up_grad, pair[1, at, :])
        for group in range(groups):
            parts[group][:, at] = value[group * rows : (group + 1) * rows].astype(
                parts[group].dtype
            )


def expert_rows(toks, cots, pair, down):
    groups = len(toks)
    rows, width = toks[0].shape
    units = down.shape[0]
    chunk = min(512, width)
    total = groups * rows
    whole = pl.BlockSpec(memory_space=pltpu.VMEM)
    out_shape = [jax.ShapeDtypeStruct((total, units), jnp.bfloat16)] * 3
    out_shape += [
        jax.ShapeDtypeStruct((rows, width), jnp.float32 if group == 0 else jnp.bfloat16)
        for group in range(groups)
    ]
    out = pl.pallas_call(
        functools.partial(expert_kernel, groups, chunk),
        in_specs=[whole] * (2 * groups) + [pl.BlockSpec(memory_space=pl.ANY)] * 2,
        out_specs=[whole] * len(out_shape),
        out_shape=out_shape,
        scratch_shapes=[
            pltpu.VMEM(pair.shape, jnp.bfloat16),
            pltpu.VMEM(down.shape, jnp.bfloat16),
            pltpu.VMEM((total, width), jnp.bfloat16),
            pltpu.VMEM((total, width), jnp.bfloat16),
            pltpu.VMEM((total, units), jnp.float32),
            pltpu.VMEM((total, units), jnp.float32),
            pltpu.VMEM((total, units), jnp.float32),
            pltpu.SemaphoreType.DMA((2, width // chunk)),
        ],
        compiler_params=pltpu.CompilerParams(vmem_limit_bytes=48 * MIB),
        cost_estimate=cost(10 * total * width * units, 6 * width * units),
        name="expert_rows",
    )(*toks, *cots, pair, down)
    return out[0], out[1], out[2], out[3:]


def pair_grad_kernel(groups, *refs):
    gate_ref, up_ref = refs[groups : groups + 2]
    out_ref = refs[groups + 2]
    tok = jnp.concatenate([ref[...] for ref in refs[:groups]], axis=0)
    out_ref[0, 0] = dot_tn(tok, gate_ref[...]).astype(jnp.bfloat16)
    out_ref[0, 1] = dot_tn(tok, up_ref[...]).astype(jnp.bfloat16)


def pair_grad(toks, gate_grad, up_grad):
    groups = len(toks)
    rows, width = toks[0].shape
    total, units = gate_grad.shape
    tile = min(512, width)
    return pl.pallas_call(
        functools.partial(pair_grad_kernel, groups),
        grid=(width // tile,),
        in_specs=[pl.BlockSpec((rows, tile), lambda c: (0, c))] * groups
        + [pl.BlockSpec((total, units), lambda c: (0, 0))] * 2,
        out_specs=pl.BlockSpec((1, 2, tile, units), lambda c: (0, 0, c, 0)),
        out_shape=jax.ShapeDtypeStruct((1, 2, width, units), jnp.bfloat16),
        compiler_params=pltpu.CompilerParams(vmem_limit_bytes=24 * MIB),
        cost_estimate=cost(4 * total * width * units, 4 * width * units),
        name="pair_grad",
    )(*toks, gate_grad, up_grad)


def down_grad_kernel(groups, *refs):
    hidden_ref, out_ref = refs[groups], refs[groups + 1]
    cot = jnp.concatenate([ref[...] for ref in refs[:groups]], axis=0)
    out_ref[0] = dot_tn(hidden_ref[...], cot).astype(jnp.bfloat16)


def down_grad(cots, hidden):
    groups = len(cots)
    rows, width = cots[0].shape
    total, units = hidden.shape
    tile = min(512, width)
    return pl.pallas_call(
        functools.partial(down_grad_kernel, groups),
        grid=(width // tile,),
        in_specs=[pl.BlockSpec((rows, tile), lambda c: (0, c))] * groups
        + [pl.BlockSpec((total, units), lambda c: (0, 0))],
        out_specs=pl.BlockSpec((1, units, tile), lambda c: (0, 0, c)),
        out_shape=jax.ShapeDtypeStruct((1, units, width), jnp.bfloat16),
        compiler_params=pltpu.CompilerParams(vmem_limit_bytes=24 * MIB),
        cost_estimate=cost(2 * total * width * units, 2 * width * units),
        name="down_grad",
    )(*cots, hidden)


def per_device(activations, cotangent, expert_ids, gate_probs, gate_up, down_proj):
    experts = lax.axis_size("expert")
    groups = lax.axis_size("dp")
    tokens, width = activations.shape
    send, place = route(
        expert_ids.reshape(1, tokens), gate_probs.reshape(1, tokens), activations, cotangent, experts
    )
    got = lax.all_to_all(send, "expert", split_axis=0, concat_axis=0, tiled=True)
    own_tok = got[:, :CAP].reshape(experts * CAP, width)
    own_cot = got[:, CAP:].reshape(experts * CAP, width)

    def shift(value, by):
        return lax.ppermute(value, "dp", [(i, (i + by) % groups) for i in range(groups)])

    toks = [own_tok] + [shift(own_tok, by) for by in range(1, groups)]
    cots = [own_cot] + [shift(own_cot, by) for by in range(1, groups)]
    gate_grad, up_grad, hidden, parts = expert_rows(toks, cots, gate_up[0], down_proj[0])
    summed = parts[0]
    for by in range(1, groups):
        summed = summed + shift(parts[by], -by).astype(jnp.float32)
    rounded = summed.astype(jnp.bfloat16).reshape(experts, CAP, width)
    returned = lax.all_to_all(rounded, "expert", split_axis=0, concat_axis=0, tiled=True)
    pair_total = pair_grad(toks, gate_grad, up_grad)
    down_total = down_grad(cots, hidden)
    input_grad = dot_tn(place, returned.reshape(experts * CAP, width)).astype(jnp.bfloat16)
    return input_grad, pair_total, down_total


def solution(mesh):
    rows = P(("dp", "expert"), None)
    pair, down = P("expert", None, None, "dp"), P("expert", "dp", None)
    return jax.shard_map(
        per_device,
        mesh=mesh,
        in_specs=(rows, rows, rows, rows, pair, down),
        out_specs=(rows, pair, down),
        check_vma=False,
    )
```

time: 122 us -> 81.7 us (0.67)
  matrix products: 40.2 us -> 1.43 us
  Pallas kernels: 0 us -> 26.1 us
  other arithmetic: 14.1 us -> 0.05 us
  between operations: 14.1 us -> 0.7 us
  starting transfers between devices: 16.6 us -> 8.44 us
  blocking collectives: 17.7 us -> 21.6 us
  local copies, waits for them, and re-layouts: 2.98 us -> 5.49 us
  waiting for transfers between devices: 15.5 us -> 17.5 us
    dot_general x11 -> x1, matrix products: 40.2 us -> 1.43 us  [dot_tn(): lax.dot_general(a, b, (((0,), (0,)), ((), ())), preferred_element_type=jn...]
    pallas_call x0 -> x4, Pallas kernels: none -> 26.1 us  [the longest x1 11.3 us: expert_rows(): pl.pallas_call(functools.partial(expert_kernel, groups, chunk), in_specs=...]
    all_to_all x0 -> x1, blocking collectives: none -> 21.6 us  [per_device(): lax.all_to_all(send, 'expert', split_axis=0, concat_axis=0, tiled=True)]
    all_gather x2 -> x0, blocking collectives: 17.7 us -> none  [the longest x1 9.17 us: per_device(): lax.all_gather(got_tok, 'dp', axis=0, tiled=True)]
    ppermute x0 -> x3, waiting for transfers between devices: none -> 17.5 us  [shift(): lax.ppermute(value, 'dp', [(i, (i + by) % groups) for i in range(groups)])]
    all_to_all x2 -> x0, starting transfers between devices: 10.9 us -> none  [the longest x1 7.36 us: per_device(): lax.all_to_all(send_tok, 'expert', split_axis=0, concat_axis=0, tiled=True)]
    another operation x2 -> x0, other arithmetic: 10.7 us -> none  [the longest x1 10.5 us: expert_rows(): return (jnp.stack([total_gate, total_up]), total_down, input_all)]
    reduce_scatter x1 -> x0, waiting for transfers between devices: 7.96 us -> none  [per_device(): lax.psum_scatter(partial_value, 'dp', scatter_dimension=0, tiled=True)]
  transfers between devices with their start and end apart: 4 -> 4, of which waited for: 2 -> 3; matrix products, arithmetic and copies ran while one was open for 28% -> 0% of each run, Pallas kernels for 0% -> 16%
where the time goes in v1:
time: 81.7 us; the launch traced here: 81.3 us
  Pallas kernels  26.1 us (32%)
  blocking collectives  21.6 us (26%)
  waiting for transfers between devices  17.5 us (21%)
  starting transfers between devices  8.44 us (10%)
  local copies, waits for them, and re-layouts  5.49 us (7%)
  matrix products  1.43 us (2%)
    all_to_all x1, blocking collectives, per_device(): lax.all_to_all(send, 'expert', split_axis=0, concat_axis=0, tiled=True)  21.6 us
    ppermute x3, waiting for transfers between devices, shift(): lax.ppermute(value, 'dp', [(i, (i + by) % groups) for i in range(groups)])  17.5 us
    pallas_call x1, Pallas kernels, expert_rows(): pl.pallas_call(functools.partial(expert_kernel, groups, chunk), in_specs=...  11.3 us
    pallas_call x1, Pallas kernels, pair_grad(): pl.pallas_call(functools.partial(pair_grad_kernel, groups), grid=(width /...  7.58 us
    pallas_call x1, Pallas kernels, down_grad(): pl.pallas_call(functools.partial(down_grad_kernel, groups), grid=(width /...  5.52 us
    all_to_all x1, starting transfers between devices, per_device(): lax.all_to_all(rounded, 'expert', split_axis=0, concat_axis=0, tiled=True)  4.71 us
    unnamed x8, local copies, waits for them, and re-layouts  3.75 us
    ppermute x3, starting transfers between devices, shift(): lax.ppermute(value, 'dp', [(i, (i + by) % groups) for i in range(groups)])  3.73 us
  transfers between devices with their start and end apart: 4, of which 3 were waited for; matrix products, arithmetic and copies ran while one was open for 0% of the time, Pallas kernels for 16%

profile of v1, /device:TPU:0, one launch (start us, length us, event | category | flops | bytes accessed | tf_op | source)
XLA Modules:
  0.0 81.3 jit_solution(8249901073868784078)
XLA Ops:
  0.6 0.0 copy-start
  0.6 1.2 %copy-done = bf16[128,4096]{1,0:T(8,128)(2,1)S(1)} copy-done((bf16[128,4096]{1,0:T(8,128)(2,1)S(1)}, bf16[128,4096]{1,0:T(8,128)(2,1)}, u32[]{:S(2)}) %copy-start) | copy-done | bytes 1048600
  1.9 1.2 %copy-done.1 = bf16[128,4096]{1,0:T(8,128)(2,1)S(1)} copy-done((bf16[128,4096]{1,0:T(8,128)(2,1)S(1)}, bf16[128,4096]{1,0:T(8,128)(2,1)}, u32[]{:S(2)}) %copy-start.1) | copy-done | bytes 1048600
  3.1 0.7 copy-done.2
  3.7 0.7 copy-done.3
  4.4 1.7 %route_rows.1 = (bf16[16,4,4096]{2,1,0:T(4,128)(2,1)S(1)}, bf16[32,128]{1,0:T(8,128)(2,1)S(1)}) custom-call(s32[1,128]{1,0:T(1,128)S(1)} %bitcast.6, f32[1,128]{1,0:T(1,128)S(1)} %bitcast.7, bf16[128,4096]{1,0:T(8,128)(2,1)S(1)} %copy-done, bf16[128,4096]{1,0:T(8,128)(2,1)S(1)} %copy-done.1), custom_call_target="tpu_custom_call" | custom-call | flops 67108864 | bytes 2097152 | tf_op jit(solution)/shard_map/route_rows/pallas_call | solution.py:59
  6.1 21.6 %all_to_all.10 = bf16[16,4,4096]{2,1,0:T(4,128)(2,1)S(1)} all-to-all(bf16[16,4,4096]{2,1,0:T(4,128)(2,1)S(1)} %get-tuple-element.11), channel_id=1, replica_groups=mesh['dp'=2,'expert'=16] {'expert'}, dimensions={0} | all-to-all | bytes 1048576 | tf_op jit(solution)/shard_map/all_to_all | solution.py:226
  27.7 0.5 fusion
  28.3 0.1 reshape.26.refs_0_
  28.4 1.6 %collective-permute-start = (bf16[32,4096]{1,0:T(8,128)(2,1)S(1)}, bf16[32,4096]{1,0:T(8,128)(2,1)S(1)}, u32[]{:S(2)}, u32[]{:S(2)}) collective-permute-start(bf16[32,4096]{1,0:T(8,128)(2,1)S(1)} %reshape.26.refs_0_), channel_id=1, source_target_pairs={{0,16},{16,0},{1,17},{17,1},{2,18},{18,2},{3,19},{19,3},{4,20},{20... | collective-permute-start | bytes 786440 | tf_op jit(solution)/shard_map/ppermute | solution.py:231
  30.0 0.1 reshape.27.refs_2_.refs_0_
  30.1 0.6 collective-permute-start.1
  30.6 7.0 %collective-permute-done.refs_1_ = bf16[32,4096]{1,0:T(8,128)(2,1)S(1)} collective-permute-done((bf16[32,4096]{1,0:T(8,128)(2,1)S(1)}, bf16[32,4096]{1,0:T(8,128)(2,1)S(1)}, u32[]{:S(2)}, u32[]{:S(2)}) %collective-permute-start) | collective-permute-done | bytes 262176 | tf_op jit(solution)/shard_map/ppermute | solution.py:231
  37.6 4.7 %collective-permute-done.1.refs_3_.refs_1_ = bf16[32,4096]{1,0:T(8,128)(2,1)S(1)} collective-permute-done((bf16[32,4096]{1,0:T(8,128)(2,1)S(1)}, bf16[32,4096]{1,0:T(8,128)(2,1)S(1)}, u32[]{:S(2)}, u32[]{:S(2)}) %collective-permute-start.1) | collective-permute-done | bytes 262176 | tf_op jit(solution)/shard_map/ppermute | solution.py:231
  42.3 11.3 %expert_rows.1 = (bf16[64,768]{1,0:T(8,128)(2,1)S(1)}, bf16[64,768]{1,0:T(8,128)(2,1)S(1)}, bf16[64,768]{1,0:T(8,128)(2,1)S(1)}, f32[32,4096]{1,0:T(8,128)S(1)}, bf16[32,4096]{1,0:T(8,128)(2,1)S(1)}) custom-call(bf16[32,4096]{1,0:T(8,128)(2,1)S(1)} %reshape.26.refs_0_, bf16[32,4096]{1,0:T(8,128)(2,1)S(1)} %collective-permute-done.refs_1_, ...), custom_call_target="tpu_custom_call" | custom-call | flops 2013265920 | bytes 18874368 | tf_op jit(solution)/shard_map/expert_rows/pallas_call | solution.py:147
  53.6 1.6 %collective-permute-start.2 = (bf16[32,4096]{1,0:T(8,128)(2,1)S(1)}, bf16[32,4096]{1,0:T(8,128)(2,1)S(1)}, u32[]{:S(2)}, u32[]{:S(2)}) collective-permute-start(bf16[32,4096]{1,0:T(8,128)(2,1)S(1)} %get-tuple-element.13), channel_id=1, source_target_pairs={{0,16},{16,0},{1,17},{17,1},{2,18},{18,2},{3,19},{19,3},{4,20},{20... | collective-permute-start | bytes 786440 | tf_op jit(solution)/shard_map/ppermute | solution.py:231
  55.2 5.9 %collective-permute-done.2 = bf16[32,4096]{1,0:T(8,128)(2,1)S(1)} collective-permute-done((bf16[32,4096]{1,0:T(8,128)(2,1)S(1)}, bf16[32,4096]{1,0:T(8,128)(2,1)S(1)}, u32[]{:S(2)}, u32[]{:S(2)}) %collective-permute-start.2) | collective-permute-done | bytes 262176 | tf_op jit(solution)/shard_map/ppermute | solution.py:231
  61.1 0.9 %reshape.28 = bf16[16,2,4096]{2,1,0:T(2,128)(2,1)} reshape(bf16[32,4096]{1,0:T(8,128)(2,1)S(1)} %add_convert_fusion) | data formatting | bytes 524288 | tf_op jit(solution)/shard_map/reshape | solution.py:239
  62.0 4.7 %all-to-all-start.1 = ((bf16[16,2,4096]{2,1,0:T(2,128)(2,1)}), bf16[16,2,4096]{2,1,0:T(2,128)(2,1)S(1)}, u32[]{:S(2)}, u32[]{:S(2)}) async-start(bf16[16,2,4096]{2,1,0:T(2,128)(2,1)} %reshape.28), calls=%async_computation.1 | async-start | bytes 524288 | tf_op jit(solution)/shard_map/all_to_all | solution.py:240
  66.7 5.5 %down_grad.1 = bf16[1,768,4096]{2,1,0:T(8,128)(2,1)} custom-call(bf16[32,4096]{1,0:T(8,128)(2,1)S(1)} %reshape.27.refs_2_.refs_0_, bf16[32,4096]{1,0:T(8,128)(2,1)S(1)} %collective-permute-done.1.refs_3_.refs_1_, bf16[64,768]{1,0:T(8,128)(2,1)S(1)} %get-tuple-element.16.refs_2_), custom_call_target="tpu_custom_call" | custom-call | flops 402653184 | bytes 6291456 | tf_op jit(solution)/shard_map/down_grad/pallas_call | solution.py:206
  72.2 7.6 %pair_grad.1 = bf16[1,2,4096,768]{3,2,1,0:T(8,128)(2,1)} custom-call(bf16[32,4096]{1,0:T(8,128)(2,1)S(1)} %reshape.26.refs_0_, bf16[32,4096]{1,0:T(8,128)(2,1)S(1)} %collective-permute-done.refs_1_, bf16[64,768]{1,0:T(8,128)(2,1)S(1)} %get-tuple-element.14.refs_2_, bf16[64,768]{1,0:T(8,128)(2,1)S(1)} %get-tuple-element.15.refs_3_), custom_call_target="tpu_custom_call" | custom-call | flops 805306368 | bytes 12582912 | tf_op jit(solution)/shard_map/pair_grad/pallas_call | solution.py:182
  79.8 0.0 all-to-all-done.1
  79.8 0.1 reshape.29
  79.9 1.4 %convolution_convert_fusion = bf16[128,4096]{1,0:T(8,128)(2,1)} fusion(bf16[32,128]{1,0:T(8,128)(2,1)S(1)} %get-tuple-element.10, bf16[32,4096]{1,0:T(8,128)(2,1)S(1)} %reshape.29), kind=kOutput, calls=%fused_computation | convolution fusion | flops 34078720 | bytes 1318912 | tf_op jit(solution)/shard_map/dot_general | solution.py:23
  (4 shorter events, 0.1 us)
Async XLA Ops:
  0.6 1.2 %copy-start = (bf16[128,4096]{1,0:T(8,128)(2,1)S(1)}, bf16[128,4096]{1,0:T(8,128)(2,1)}, u32[]{:S(2)}) copy-start(bf16[128,4096]{1,0:T(8,128)(2,1)} %act_ref.1) | copy-start | bytes 3145732
  1.9 1.2 %copy-start.1 = (bf16[128,4096]{1,0:T(8,128)(2,1)S(1)}, bf16[128,4096]{1,0:T(8,128)(2,1)}, u32[]{:S(2)}) copy-start(bf16[128,4096]{1,0:T(8,128)(2,1)} %cot_ref.1) | copy-start | bytes 3145732
  3.1 0.7 copy-start.2
  3.7 0.7 copy-start.3
  28.4 9.2 %collective-permute-start = (bf16[32,4096]{1,0:T(8,128)(2,1)S(1)}, bf16[32,4096]{1,0:T(8,128)(2,1)S(1)}, u32[]{:S(2)}, u32[]{:S(2)}) collective-permute-start(bf16[32,4096]{1,0:T(8,128)(2,1)S(1)} %reshape.26.refs_0_), channel_id=1, source_target_pairs={{0,16},{16,0},{1,17},{17,1},{2,18},{18,2},{3,19},{19,3},{4,20},{20... | collective-permute-start | bytes 786440 | tf_op jit(solution)/shard_map/ppermute | solution.py:231
  30.1 12.2 %collective-permute-start.1 = (bf16[32,4096]{1,0:T(8,128)(2,1)S(1)}, bf16[32,4096]{1,0:T(8,128)(2,1)S(1)}, u32[]{:S(2)}, u32[]{:S(2)}) collective-permute-start(bf16[32,4096]{1,0:T(8,128)(2,1)S(1)} %reshape.27.refs_2_.refs_0_), channel_id=1, source_target_pairs={{0,16},{16,0},{1,17},{17,1},{2,18},{18,2},{3,19},{19,3},{4,20},{20... | collective-permute-start | bytes 786440 | tf_op jit(solution)/shard_map/ppermute | solution.py:231
  53.6 7.4 %collective-permute-start.2 = (bf16[32,4096]{1,0:T(8,128)(2,1)S(1)}, bf16[32,4096]{1,0:T(8,128)(2,1)S(1)}, u32[]{:S(2)}, u32[]{:S(2)}) collective-permute-start(bf16[32,4096]{1,0:T(8,128)(2,1)S(1)} %get-tuple-element.13), channel_id=1, source_target_pairs={{0,16},{16,0},{1,17},{17,1},{2,18},{18,2},{3,19},{19,3},{4,20},{20... | collective-permute-start | bytes 786440 | tf_op jit(solution)/shard_map/ppermute | solution.py:231
  62.0 17.8 %all-to-all-start.1 = ((bf16[16,2,4096]{2,1,0:T(2,128)(2,1)}), bf16[16,2,4096]{2,1,0:T(2,128)(2,1)S(1)}, u32[]{:S(2)}, u32[]{:S(2)}) async-start(bf16[16,2,4096]{2,1,0:T(2,128)(2,1)} %reshape.28), calls=%async_computation.1 | async-start | bytes 524288 | tf_op jit(solution)/shard_map/all_to_all | solution.py:240
